TPU v7x, 256 devices: a whole 4x4x8 slice. The times are simulated.
256 devices in a mesh: surf: 64 (over x, z, core), col: 4 (over y).
Axes of the slice: x: 4, y: 4, z: 8, core: 2. Of those that a mesh axis runs over, the one named last changes fastest.
Arguments:
- stiffness: float32 [256, 3, 512, 512], P(('surf', 'col'))
- load: float32 [256, 3, 512, 256], P(('surf', 'col')), may hold values from -6 to 6
- start: float32 [256, 3, 512, 256], P(('surf', 'col')), may hold values from -6 to 6
- boundary_matrix: float32 [4096, 4, 16384], P('surf', None, 'col'), may hold values from -0.046875 to 0.046875
- bem_node: int32 [4, 4096], P('col'), may hold values from 0 to 4095, as said below
Outputs:
- solution_field: float32 [256, 3, 512, 256], P(('surf', 'col'))
- traction: float32 [4, 4096, 256], P('col', 'surf')
Inputs may be any that keep to these rules, and one draw needn't show every extreme that they name: Each row bem_node[g] is a permutation of 0 to 4096 - 1 (the top face nodes of column group g). For each block of 64 slots q in [s * 64, (s + 1) * 64) and each patch s2 of the group, the block's slots name either exactly 1 node of patch s2 or none; each patch's top face nodes lie in exactly 64 blocks.
All inputs are finite; a program needn't handle non-finite values.
Results may differ from a plain program's by a relative error of at most 0.0001.
Values sent between devices are 32-bit elements; how exact they have to be, the bound alone decides.
A program may use at most 128 MiB of HBM per device.

v0:
```python
import jax
import jax.numpy as jnp
from jax import lax
from jax.sharding import PartitionSpec as P

EDGE = 8
ITERS = 2


damping = 0.25
coupling = 0.5


def with_halo(block, sides, width):
    for axis, dim in sides:
        count = lax.axis_size(axis)
        forward = [(i, i + 1) for i in range(count - 1)]
        backward = [(target, source) for source, target in forward]
        low = lax.ppermute(
            lax.slice_in_dim(block, block.shape[dim] - width, None, axis=dim), axis, forward
        )
        high = lax.ppermute(lax.slice_in_dim(block, 0, width, axis=dim), axis, backward)
        block = jnp.concatenate([low, block, high], axis=dim)
    return block


def volume_apply(current, kmats, edge_cells, layers_deep, fields):
    highest = lax.Precision.HIGHEST
    cube = current.reshape(layers_deep, edge_cells, edge_cells, edge_cells, fields)
    padded = with_halo(cube, (("surf", 1), ("col", 2)), 1)
    extra = jnp.zeros_like(cube)
    extra = extra.at[:, 0].add(cube[:, 0] - padded[:, 0, 1:-1])
    extra = extra.at[:, -1].add(cube[:, -1] - padded[:, -1, 1:-1])
    extra = extra.at[:, :, 0].add(cube[:, :, 0] - padded[:, 1:-1, 0])
    extra = extra.at[:, :, -1].add(cube[:, :, -1] - padded[:, 1:-1, -1])
    low_k = cube[:, :, :, 0]
    high_k = cube[:, :, :, -1]
    deeper = jnp.concatenate([low_k[1:], jnp.zeros_like(low_k[:1])], axis=0)
    extra = extra.at[:, :, :, -1].add(high_k - deeper)
    extra = extra.at[1:, :, :, 0].add(low_k[1:] - high_k[:-1])
    applied = jnp.einsum("dab,dbf->daf", kmats, current, precision=highest)
    return applied.reshape(cube.shape) + coupling * extra


def shards(stiffness, load, start, boundary_matrix, bem_node):
    highest = lax.Precision.HIGHEST
    my_index = lax.axis_index("surf")
    layers_deep = stiffness.shape[1]
    node_count = stiffness.shape[2]
    fields = load.shape[3]
    edge_cells = EDGE
    face_nodes = edge_cells * edge_cells
    group_map = bem_node[0]
    group_size = group_map.shape[0]
    slot_of_node = jnp.argsort(group_map)
    kmats = stiffness[0]
    load_cube = load[0].reshape(layers_deep, edge_cells, edge_cells, edge_cells, fields)
    operator_rows = boundary_matrix.reshape(-1, group_size)
    my_node_slots = lax.dynamic_slice_in_dim(slot_of_node, my_index * face_nodes, face_nodes)
    current = start[0]
    traction_rows = jnp.zeros((face_nodes, fields), jnp.float32)
    for turn_index in range(ITERS):
        cube = current.reshape(layers_deep, edge_cells, edge_cells, edge_cells, fields)
        top_face = cube[0, :, :, 0, :].reshape(face_nodes, fields)
        gathered = lax.all_gather(top_face, "surf", axis=0, tiled=True)
        ordered = jnp.take(gathered, group_map, axis=0)
        partial_value = jnp.dot(
            operator_rows, ordered, precision=highest, preferred_element_type=jnp.float32
        )
        summed = lax.psum_scatter(
            partial_value.reshape(face_nodes, -1, fields), "col", scatter_dimension=1, tiled=True
        )
        traction_rows = summed.reshape(face_nodes, fields)
        all_rows = lax.all_gather(traction_rows, "surf", axis=0, tiled=True)
        on_top = jnp.take(all_rows, my_node_slots, axis=0)
        applied = volume_apply(current, kmats, edge_cells, layers_deep, fields)
        applied = applied.at[0, :, :, 0, :].add(on_top.reshape(edge_cells, edge_cells, fields))
        residual = load_cube - applied
        current = (cube + damping * residual).reshape(layers_deep, node_count, fields)
    return (current[None], traction_rows[None])


def solution(mesh):
    in_specs = (
        P(("surf", "col"), None, None, None),
        P(("surf", "col"), None, None, None),
        P(("surf", "col"), None, None, None),
        P("surf", None, "col"),
        P("col", None),
    )
    out_specs = (P(("surf", "col"), None, None, None), P("col", "surf", None))
    return jax.shard_map(shards, mesh=mesh, in_specs=in_specs, out_specs=out_specs, check_vma=False)
```

profile of v0, /device:TPU:1, one launch (start us, length us, event | category | flops | bytes accessed | tf_op | source)
XLA Modules:
  0.0 461.6 jit_solution(13681945095157023550)
XLA Ops:
  9.2 5.3 %reshape.595 = f32[256,4096]{1,0:T(8,128)} reshape(f32[64,4,4096]{2,1,0:T(4,128)} %param.40) | data formatting | bytes 8388608 | tf_op jit(solution)/shard_map/reshape | solution.py:58
  14.5 80.1 %all-gather.7.cloned.1.call-done = f32[4096,256]{1,0:T(8,128)} async-done(((f32[64,256]{1,0:T(8,128)}), f32[4096,256]{1,0:T(8,128)}) %all-gather.7.cloned.1.call-update) | async-done | bytes 4194320 | tf_op jit(solution)/shard_map/all_gather | solution.py:65
  94.6 18.3 %gather_fusion = f32[4096,256]{1,0:T(8,128)} fusion(f32[4096,256]{1,0:T(8,128)} %all-gather.7.cloned.1.call-done, s32[4096]{0:T(1024)S(1)} %fusion.36), kind=kCustom, calls=%fused_computation.clone | custom fusion | bytes 8404992 | tf_op jit(solution)/shard_map/jit(_take)/gather | solution.py:66
  112.9 7.4 %fusion.16 = f32[256,256]{1,0:T(8,128)S(1)} fusion(f32[256,4096]{1,0:T(8,128)} %reshape.595, f32[4096,256]{1,0:T(8,128)} %gather_fusion, pred[4096]{0:T(1024)(128)(4,1)S(1)} %compare_and_fusion), kind=kOutput, calls=%fused_computation.22 | convolution fusion | flops 3222274048 | bytes 8654848 | tf_op jit(solution)/shard_map/dot_general | solution.py:67
  122.8 17.9 %reduce-scatter.3.cloned.1.call-done = f32[64,1,256]{2,0,1:T(8,128)} async-done(((f32[64,4,256]{2,0,1:T(8,128)}), f32[64,1,256]{2,0,1:T(8,128)}) %reduce-scatter.3.cloned.1.call-update) | async-done | bytes 65552 | tf_op jit(solution)/shard_map/reduce_scatter | solution.py:70
  142.8 6.2 %collective-permute-start = (f32[3,1,8,8,256]{4,2,1,0,3:T(8,128)S(1)}, f32[3,1,8,8,256]{4,2,1,0,3:T(8,128)S(1)}, u32[]{:S(2)}, u32[]{:S(2)}) collective-permute-start(f32[3,1,8,8,256]{4,2,1,0,3:T(8,128)S(1)} %slice.588), channel_id=1, source_target_pairs={{0,4},{4,8},{8,12},{12,16},{16,20},{20,24},{24,28},{28,32},{32,36}... | collective-permute-start | bytes 589832 | tf_op jit(solution)/shard_map/ppermute | solution.py:19
  155.4 4.0 collective-permute-done.1
  163.2 4.0 fusion.6
  167.3 5.8 %sort.17 = (s32[4096]{0:T(1024)}, s32[4096]{0:T(1024)S(1)}) sort(s32[4096]{0:T(1024)S(1)} %bitcast.95, s32[4096]{0:T(1024)S(1)} %iota.4), dimensions={0}, to_apply=%region_1.3 | sort | flops 49152 | bytes 65536 | tf_op jit(solution)/shard_map/jit(argsort)/sort | solution.py:55
  176.9 4.5 scatter-add.50
  183.8 4.5 scatter-add.51
  190.9 3.5 copy.36
  196.2 4.0 scatter-add.55
  200.2 3.4 multiply_add_fusion.3
  203.7 22.6 %all-gather.11.cloned.1.call-done = f32[4096,1,256]{2,0,1:T(8,128)} async-done(((f32[64,1,256]{2,0,1:T(8,128)}), f32[4096,1,256]{2,0,1:T(8,128)}) %all-gather.11.cloned.1.call-update) | async-done | bytes 4194320 | tf_op jit(solution)/shard_map/all_gather | solution.py:74
  226.3 2.8 gather_fusion.1
  237.3 76.4 %all-gather.9.cloned.1.call-done = f32[4096,256]{1,0:T(8,128)} async-done(((f32[64,256]{1,0:T(8,128)}), f32[4096,256]{1,0:T(8,128)}) %all-gather.9.cloned.1.call-update) | async-done | bytes 4194320 | tf_op jit(solution)/shard_map/all_gather | solution.py:65
  313.7 18.3 %gather_fusion.2 = f32[4096,256]{1,0:T(8,128)} fusion(f32[4096,256]{1,0:T(8,128)} %all-gather.9.cloned.1.call-done, s32[4096]{0:T(1024)S(1)} %fusion.36), kind=kCustom, calls=%fused_computation.2.clone | custom fusion | bytes 8404992 | tf_op jit(solution)/shard_map/jit(_take)/gather | solution.py:66
  332.0 7.4 %fusion.19 = f32[256,256]{1,0:T(8,128)S(1)} fusion(f32[256,4096]{1,0:T(8,128)} %reshape.595, f32[4096,256]{1,0:T(8,128)} %gather_fusion.2, pred[4096]{0:T(1024)(128)(4,1)S(1)} %compare_and_fusion), kind=kOutput, calls=%fused_computation.23 | convolution fusion | flops 3222274048 | bytes 8654848 | tf_op jit(solution)/shard_map/dot_general | solution.py:67
  341.9 17.9 %reduce-scatter.5.cloned.1.call-done = f32[64,1,256]{2,0,1:T(8,128)} async-done(((f32[64,4,256]{2,0,1:T(8,128)}), f32[64,1,256]{2,0,1:T(8,128)}) %reduce-scatter.5.cloned.1.call-update) | async-done | bytes 65552 | tf_op jit(solution)/shard_map/reduce_scatter | solution.py:70
  361.9 6.2 %collective-permute-start.4 = (f32[3,1,8,8,256]{4,2,1,0,3:T(8,128)S(1)}, f32[3,1,8,8,256]{4,2,1,0,3:T(8,128)S(1)}, u32[]{:S(2)}, u32[]{:S(2)}) collective-permute-start(f32[3,1,8,8,256]{4,2,1,0,3:T(8,128)S(1)} %slice.605), channel_id=1, source_target_pairs={{0,4},{4,8},{8,12},{12,16},{16,20},{20,24},{24,28},{28,32},{32,36}... | collective-permute-start | bytes 589832 | tf_op jit(solution)/shard_map/ppermute | solution.py:19
  374.4 4.0 collective-permute-done.5
  382.2 6.6 %fusion.13 = f32[3,512,256]{1,2,0:T(8,128)} fusion(f32[3,512,256]{2,1,0:T(8,128)S(1)} %bitcast.77, f32[1,3,512,512]{3,2,1,0:T(8,128)S(1)} %copy-done), kind=kOutput, calls=%fused_computation.21 | convolution fusion | flops 2415919104 | bytes 6291456 | tf_op jit(solution)/shard_map/dab,dbf->daf/dot_general | solution.py:41
  389.5 3.0 copy.40
  396.8 4.5 scatter-add.61
  403.1 4.5 scatter-add.64
  410.4 3.5 copy.48
  415.7 4.0 scatter-add.66
  419.7 3.4 multiply_add_fusion.1
  423.2 21.3 %all-gather.13.cloned.1.call-done = f32[4096,1,256]{2,0,1:T(8,128)} async-done(((f32[64,1,256]{2,0,1:T(8,128)}), f32[4096,1,256]{2,0,1:T(8,128)}) %all-gather.13.cloned.1.call-update) | async-done | bytes 4194320 | tf_op jit(solution)/shard_map/all_gather | solution.py:74
  444.5 2.8 gather_fusion.3
  450.8 3.9 multiply_add_fusion
  (87 shorter events, 65.0 us)
Async XLA Ops:
  7.2 156.0 %copy-start = (f32[1,3,512,512]{3,2,1,0:T(8,128)S(1)}, f32[1,3,512,512]{3,2,1,0:T(8,128)}, u32[]{:S(2)}) copy-start(f32[1,3,512,512]{3,2,1,0:T(8,128)} %param.37) | copy-start | bytes 9437188
  7.2 87.4 %all-gather.7.cloned.1.call-start = ((), (), s32[]{:S(2)}) async-start(), calls=%async_computation.2 | async-start | bytes 4259840 | tf_op jit(solution)/shard_map/all_gather | solution.py:65
  9.1 5.3 %copy-start.6 = (s32[1,4096]{1,0:T(1,128)S(1)}, s32[1,4096]{1,0:T(1,128)}, u32[]{:S(2)}) copy-start(s32[1,4096]{1,0:T(1,128)} %param.41) | copy-start | bytes 49156
  9.1 131.6 %reduce-scatter.3.cloned.1.call-start = ((), (), s32[]{:S(2)}) async-start(), calls=%async_computation.3 | async-start | bytes 327680 | tf_op jit(solution)/shard_map/reduce_scatter | solution.py:70
  122.8 103.5 %all-gather.11.cloned.1.call-start = ((), (), s32[]{:S(2)}) async-start(), calls=%async_computation.6 | async-start | bytes 4259840 | tf_op jit(solution)/shard_map/all_gather | solution.py:74
  140.8 172.9 %all-gather.9.cloned.1.call-start = ((), (), s32[]{:S(2)}) async-start(), calls=%async_computation.4 | async-start | bytes 4259840 | tf_op jit(solution)/shard_map/all_gather | solution.py:65
  142.7 16.6 %copy-start.4 = (f32[3,8,8,8,256]{4,2,1,0,3:T(8,128)}, f32[3,8,8,8,256]{4,2,1,0,3:T(8,128)S(1)}, u32[]{:S(2)}) copy-start(f32[3,8,8,8,256]{4,2,1,0,3:T(8,128)S(1)} %copy.29) | copy-start | bytes 4718596
  142.8 12.2 %copy-start.3 = (f32[1,3,512,256]{3,2,1,0:T(8,128)S(1)}, f32[1,3,512,256]{3,2,1,0:T(8,128)}, u32[]{:S(2)}) copy-start(f32[1,3,512,256]{3,2,1,0:T(8,128)} %param.39) | copy-start | bytes 4718596
  142.8 8.8 %collective-permute-start = (f32[3,1,8,8,256]{4,2,1,0,3:T(8,128)S(1)}, f32[3,1,8,8,256]{4,2,1,0,3:T(8,128)S(1)}, u32[]{:S(2)}, u32[]{:S(2)}) collective-permute-start(f32[3,1,8,8,256]{4,2,1,0,3:T(8,128)S(1)} %slice.588), channel_id=1, source_target_pairs={{0,4},{4,8},{8,12},{12,16},{16,20},{20,24},{24,28},{28,32},{32,36}... | collective-permute-start | bytes 589832 | tf_op jit(solution)/shard_map/ppermute | solution.py:19
  151.6 7.7 %collective-permute-start.1 = (f32[3,1,8,8,256]{4,2,1,0,3:T(8,128)S(1)}, f32[3,1,8,8,256]{4,2,1,0,3:T(8,128)S(1)}, u32[]{:S(2)}, u32[]{:S(2)}) collective-permute-start(f32[3,1,8,8,256]{4,2,1,0,3:T(8,128)S(1)} %get-tuple-element.184), channel_id=1, source_target_pairs={{4,0},{8,4},{12,8},{16,12},{20,16},{24,20},{28,24},{32,28},{36,32}... | collective-permute-start | bytes 589832 | tf_op jit(solution)/shard_map/ppermute | solution.py:22
  161.2 13.4 %collective-permute-start.2 = (f32[3,10,1,8,256]{4,2,1,0,3:T(1,128)}, f32[3,10,1,8,256]{4,2,1,0,3:T(1,128)}, u32[]{:S(2)}, u32[]{:S(2)}) collective-permute-start(f32[3,10,1,8,256]{4,2,1,0,3:T(1,128)} %get-tuple-element.179), channel_id=1, source_target_pairs={{0,1},{1,2},{2,3},{4,5},{5,6},{6,7},{8,9},{9,10},{10,11},{12,13},{... | collective-permute-start | bytes 737288 | tf_op jit(solution)/shard_map/ppermute | solution.py:19
  173.1 8.3 %collective-permute-start.3 = (f32[3,10,1,8,256]{4,2,1,0,3:T(1,128)}, f32[3,10,1,8,256]{4,2,1,0,3:T(1,128)}, u32[]{:S(2)}, u32[]{:S(2)}) collective-permute-start(f32[3,10,1,8,256]{4,2,1,0,3:T(1,128)} %get-tuple-element.178), channel_id=1, source_target_pairs={{1,0},{2,1},{3,2},{5,4},{6,5},{7,6},{9,8},{10,9},{11,10},{13,12},{... | collective-permute-start | bytes 737288 | tf_op jit(solution)/shard_map/ppermute | solution.py:22
  235.4 1.1 copy-start.1
  237.2 122.6 %reduce-scatter.5.cloned.1.call-start = ((), (), s32[]{:S(2)}) async-start(), calls=%async_computation.5 | async-start | bytes 327680 | tf_op jit(solution)/shard_map/reduce_scatter | solution.py:70
  341.9 102.6 %all-gather.13.cloned.1.call-start = ((), (), s32[]{:S(2)}) async-start(), calls=%async_computation.7 | async-start | bytes 4259840 | tf_op jit(solution)/shard_map/all_gather | solution.py:74
  361.8 16.6 %copy-start.5 = (f32[3,8,8,8,256]{4,2,1,0,3:T(8,128)}, f32[3,8,8,8,256]{4,2,1,0,3:T(8,128)S(1)}, u32[]{:S(2)}) copy-start(f32[3,8,8,8,256]{4,2,1,0,3:T(8,128)S(1)} %copy.41) | copy-start | bytes 4718596
  361.8 12.2 %copy-start.2 = (f32[3,8,8,8,256]{4,3,2,1,0:T(8,128)S(1)}, f32[3,8,8,8,256]{4,3,2,1,0:T(8,128)}, u32[]{:S(2)}) copy-start(f32[3,8,8,8,256]{4,3,2,1,0:T(8,128)} %copy-done.1) | copy-start | bytes 4718596
  361.9 8.8 %collective-permute-start.4 = (f32[3,1,8,8,256]{4,2,1,0,3:T(8,128)S(1)}, f32[3,1,8,8,256]{4,2,1,0,3:T(8,128)S(1)}, u32[]{:S(2)}, u32[]{:S(2)}) collective-permute-start(f32[3,1,8,8,256]{4,2,1,0,3:T(8,128)S(1)} %slice.605), channel_id=1, source_target_pairs={{0,4},{4,8},{8,12},{12,16},{16,20},{20,24},{24,28},{28,32},{32,36}... | collective-permute-start | bytes 589832 | tf_op jit(solution)/shard_map/ppermute | solution.py:19
  370.7 7.7 %collective-permute-start.5 = (f32[3,1,8,8,256]{4,2,1,0,3:T(8,128)S(1)}, f32[3,1,8,8,256]{4,2,1,0,3:T(8,128)S(1)}, u32[]{:S(2)}, u32[]{:S(2)}) collective-permute-start(f32[3,1,8,8,256]{4,2,1,0,3:T(8,128)S(1)} %get-tuple-element.182), channel_id=1, source_target_pairs={{4,0},{8,4},{12,8},{16,12},{20,16},{24,20},{28,24},{32,28},{36,32}... | collective-permute-start | bytes 589832 | tf_op jit(solution)/shard_map/ppermute | solution.py:22
  380.3 14.7 %collective-permute-start.6 = (f32[3,10,1,8,256]{4,2,1,0,3:T(1,128)}, f32[3,10,1,8,256]{4,2,1,0,3:T(1,128)}, u32[]{:S(2)}, u32[]{:S(2)}) collective-permute-start(f32[3,10,1,8,256]{4,2,1,0,3:T(1,128)} %get-tuple-element.177), channel_id=1, source_target_pairs={{0,1},{1,2},{2,3},{4,5},{5,6},{6,7},{8,9},{9,10},{10,11},{12,13},{... | collective-permute-start | bytes 737288 | tf_op jit(solution)/shard_map/ppermute | solution.py:19
  393.6 7.6 %collective-permute-start.7 = (f32[3,10,1,8,256]{4,2,1,0,3:T(1,128)}, f32[3,10,1,8,256]{4,2,1,0,3:T(1,128)}, u32[]{:S(2)}, u32[]{:S(2)}) collective-permute-start(f32[3,10,1,8,256]{4,2,1,0,3:T(1,128)} %get-tuple-element.176), channel_id=1, source_target_pairs={{1,0},{2,1},{3,2},{5,4},{6,5},{7,6},{9,8},{10,9},{11,10},{13,12},{... | collective-permute-start | bytes 737288 | tf_op jit(solution)/shard_map/ppermute | solution.py:22
Sparse Core Ops, SparseCore 0:
  11.4 83.1 all-gather.6
  122.9 17.8 reduce-scatter.2
  143.9 82.3 all-gather.10
  237.4 76.2 all-gather.8
  342.0 17.8 reduce-scatter.4
  363.1 81.3 all-gather.12
where the time goes:
time: 463 us; the launch traced here: 462 us
  waiting for transfers between devices  250 us (54%)
  local copies, waits for them, and re-layouts  110 us (24%)
  other arithmetic  38.9 us (8%)
  matrix products  25.3 us (5%)
  starting transfers between devices  23.2 us (5%)
  between operations  14.4 us (3%)
    all_gather x2, waiting for transfers between devices, shards(): gathered = lax.all_gather(top_face, 'surf', axis=0, tiled=True)  157 us
    all_gather x2, waiting for transfers between devices, shards(): all_rows = lax.all_gather(traction_rows, 'surf', axis=0, tiled=True)  43.9 us
    gather x2, local copies, waits for them, and re-layouts, shards(): ordered = jnp.take(gathered, group_map, axis=0)  36.6 us
    reduce_scatter x2, waiting for transfers between devices, shards(): lax.psum_scatter(partial_value.reshape(face_nodes, -1, fields), 'col', sc...  35.9 us
    ppermute x4, starting transfers between devices, with_halo(): lax.ppermute(lax.slice_in_dim(block, block.shape[dim] - width, None, axis...  16.4 us
    dot_general x2, matrix products, shards(): jnp.dot(operator_rows, ordered, precision=highest, preferred_element_type...  14.7 us
    dot_general x2, matrix products, volume_apply(): applied = jnp.einsum('dab,dbf->daf', kmats, current, precision=highest)  10.6 us
  transfers between devices with their start and end apart: 14, of which 10 were waited for; matrix products, arithmetic and copies ran while one was open for 21% of the time, Pallas kernels for 0%

commit v1 on v0

v1 whole, which is shorter than its diff:
```python
import functools

import jax
import jax.numpy as jnp
from jax import lax
from jax.experimental import pallas as pl
from jax.experimental.pallas import tpu as pltpu
from jax.sharding import PartitionSpec as P

MESH = pl.DeviceIdType.MESH
F32, BF16 = jnp.float32, jnp.bfloat16
NX, NZ, NC = 4, 8, 2
EDGE, DEPTH, NODES, FACE, FIELDS = 8, 3, 512, 64, 256
GROUPS, COLS = 4, 4096
SPLIT = 24
PARTS = (pl.ds(0, SPLIT), pl.ds(SPLIT, FACE - SPLIT))
damping = 0.25
coupling = 0.5


def sign(a):
    return 1 if a > 0 else -1


def halves(a):
    high = a.astype(BF16)
    return high, (a - high.astype(F32)).astype(BF16)


def dot(a, b):
    return jnp.dot(a, b, preferred_element_type=F32)


def dot3(ah, al, bh, bl):
    return dot(ah, bh) + dot(al, bh) + dot(ah, bl)


def exact(onehot, rows):
    return jnp.dot(onehot, rows, precision=lax.Precision.HIGHEST, preferred_element_type=F32)


def kernel(
    stiff, load, start, bm, map_a, map_b, sol, trac,
    u, v, ld, uh, ul, kraw, kh, kl, mraw, mh, ml, xb, part, rsbuf, halo, tr,
    asrc, abuf, bsrc, bbuf,
    lsem, gsend, grecv, asend, arecv, rsend, rrecv, hsend, hrecv, osem,
):
    s, y = lax.axis_index("surf"), lax.axis_index("col")
    c, z, x = s % NC, (s // NC) % NZ, s // (NC * NZ)
    sgn = 1 - 2 * c
    xc = x * NC + c
    u2, v2 = u.reshape(DEPTH, NODES, FIELDS), v.reshape(DEPTH, NODES, FIELDS)

    def at(dx, dz):
        return ((x + NX + dx) % NX * NZ + (z + NZ + dz) % NZ) * NC + c

    def chip(dx, dz):
        return (x + NX + dx) % NX * NZ + (z + NZ + dz) % NZ

    sibling = s + sgn
    up, down = (s + 1) % (NX * NZ * NC), (s + NX * NZ * NC - 1) % (NX * NZ * NC)

    def mate_xc(i):
        other = (xc + i) % (NX * NC)
        return other, (other // NC * NZ + z) * NC + other % NC

    def mate_z(i):
        other = (z + i) % NZ
        return other, (x * NZ + other) * NC + c

    lead = pltpu.make_async_copy(start.at[0], u2.at[0], lsem.at[0])
    rest = pltpu.make_async_copy(start.at[pl.ds(1, 2)], u2.at[pl.ds(1, 2)], lsem.at[1])
    get_m = pltpu.make_async_copy(bm, mraw, lsem.at[2])
    get_k = pltpu.make_async_copy(stiff, kraw, lsem.at[3])
    get_l = pltpu.make_async_copy(load, ld, lsem.at[4])
    for copy in (lead, rest, get_m, get_k, get_l):
        copy.start()

    barrier = pltpu.get_barrier_semaphore()

    def greet(surf, col):
        pl.semaphore_signal(barrier, inc=1, device_id=(surf, col), device_id_type=MESH)

    for i in range(1, NX * NC):
        greet(mate_xc(i)[1], y)
    for i in range(1, NZ):
        greet(mate_z(i)[1], y)
    for i in range(1, GROUPS):
        greet(s, (y + i) % GROUPS)
    greet((s + NX * NZ * NC - sgn) % (NX * NZ * NC), y)
    pl.semaphore_wait(barrier, NX * NC - 1 + NZ - 1 + GROUPS - 1 + 1)

    sub = lax.broadcasted_iota(jnp.int32, (FACE, FACE), 0)
    lane = lax.broadcasted_iota(jnp.int32, (FACE, FACE), 1)
    ma, mb = map_a[...], map_b[...]
    mine_a = jnp.sum(jnp.where((ma >> 6) == s, ma & 63, 0), axis=1, keepdims=True)
    lane_8 = lax.broadcasted_iota(jnp.int32, (FACE, NODES), 1)
    node_out = (mine_a * EDGE == lane_8).astype(F32)
    mine_b = jnp.sum(jnp.where((mb >> 6) == s, mb & 63, 0), axis=0, keepdims=True)
    sub_8 = lax.broadcasted_iota(jnp.int32, (NODES, FACE), 0)
    node_in = (mine_b * EDGE == sub_8).astype(F32)
    row = jnp.sum(jnp.where(sub == xc * NZ + z, ma, 0), axis=0, keepdims=True) >> 6
    slot_out = (((row >> 4) * NC + (row & 1)) * NZ + ((row >> 1) & 7) == sub).astype(F32)
    column = jnp.sum(jnp.where(lane == z * (NX * NC) + xc, mb, 0), axis=1, keepdims=True) >> 6
    slot_in = (((column >> 1) & 7) * (NX * NC) + (column >> 4) * NC + (column & 1) == lane).astype(F32)

    def eight(i):
        return pl.ds(pl.multiple_of(i * 8, 8), 8)

    def rows_out(k, rows):
        for h in range(2):
            asrc[k, h] = rows[:, 128 * h : 128 * h + 128]
        abuf[k, :, eight(xc)] = asrc[k, :, eight(xc)]
        for i in range(1, NX * NC):
            other, target = mate_xc(i)
            pltpu.make_async_remote_copy(
                src_ref=asrc.at[k, :, eight(other)], dst_ref=abuf.at[k, :, eight(xc)],
                send_sem=asend.at[k, 0], recv_sem=arecv.at[k, 0],
                device_id=(target, y), device_id_type=MESH,
            ).start()

    def rows_turn(k):
        seven = abuf.at[k, :, pl.ds(0, 56)]
        pltpu.make_async_copy(seven, seven, arecv.at[k, 0]).wait()
        for h in range(2):
            for i in range(NZ):
                bsrc[k, h, pl.ds(8 * i, 8)] = abuf[k, h, pl.ds(i, 8, stride=8)]
        bbuf[k, :, eight(z)] = bsrc[k, :, eight(z)]
        for i in range(1, NZ):
            other, target = mate_z(i)
            pltpu.make_async_remote_copy(
                src_ref=bsrc.at[k, :, eight(other)], dst_ref=bbuf.at[k, :, eight(z)],
                send_sem=asend.at[k, 1], recv_sem=arecv.at[k, 1],
                device_id=(target, y), device_id_type=MESH,
            ).start()

    def rows_in(k):
        seven = bbuf.at[k, :, pl.ds(0, 56)]
        pltpu.make_async_copy(seven, seven, arecv.at[k, 1]).wait()
        return jnp.concatenate([bbuf[k, 0], bbuf[k, 1]], axis=1)

    def split_m(p):
        def go():
            for g in range(GROUPS):
                for q in range(2):
                    tile = mraw[:, g, pl.ds(256 * p + 128 * q, 128)]
                    mh[2 * p + q, pl.ds(FACE * g, FACE)], ml[2 * p + q, pl.ds(FACE * g, FACE)] = halves(tile)
        return go

    def split_k(d, r):
        def go():
            kh[d, pl.ds(128 * r, 128)], kl[d, pl.ds(128 * r, 128)] = halves(kraw[d, pl.ds(128 * r, 128)])
        return go

    def split_u(w2, d):
        def go():
            uh[d], ul[d] = halves(w2[d])
        return go

    def face_out(it, w):
        def go():
            for k, (src, target) in enumerate((
                (w.at[:, 7], (up, y)),
                (w.at[:, 0], (down, y)),
                (w.at[:, :, 7], (s, (y + 1) % GROUPS)),
                (w.at[:, :, 0], (s, (y + GROUPS - 1) % GROUPS)),
            )):
                pltpu.make_async_remote_copy(
                    src_ref=src, dst_ref=halo.at[it, k], send_sem=hsend.at[it], recv_sem=hrecv.at[it],
                    device_id=target, device_id_type=MESH,
                ).start()
        return go

    def face_in(it):
        def go():
            pltpu.make_async_copy(halo.at[it], halo.at[it], hrecv.at[it]).wait()
        return go

    low_i = jnp.where(s > 0, 1.0, 0.0).astype(F32)
    high_i = jnp.where(s < NX * NZ * NC - 1, 1.0, 0.0).astype(F32)
    low_j = jnp.where(y > 0, 1.0, 0.0).astype(F32)
    high_j = jnp.where(y < GROUPS - 1, 1.0, 0.0).astype(F32)
    weight = damping * coupling

    layer = lax.broadcasted_iota(jnp.int32, (32, EDGE, FIELDS), 1)

    def volume(w2, o2, d, r):
        def go():
            block = pl.ds(256 * r, 256)
            applied = dot3(kh[d, block], kl[d, block], uh[d], ul[d])
            here = w2[d, block].reshape(32, EDGE, FIELDS)
            term = here
            if d + 1 < DEPTH:
                term = here - pltpu.roll(w2[d + 1, block].reshape(32, EDGE, FIELDS), 7, 1)
            term = jnp.where(layer == EDGE - 1, term, 0.0)
            if d:
                above = here - pltpu.roll(w2[d - 1, block].reshape(32, EDGE, FIELDS), 1, 1)
                term = jnp.where(layer == 0, above, term)
            out = w2[d, block] + damping * (ld[d, block] - applied)
            o2[d, block] = out - weight * term.reshape(256, FIELDS)
        return go

    def faces(it, w, o, w2, o2, d):
        def go():
            o[d, 0] -= weight * (w[d, 0] - low_i * halo[it, 0, d])
            o[d, 7] -= weight * (w[d, 7] - high_i * halo[it, 1, d])
            o[d, :, 0] -= weight * (w[d, :, 0] - low_j * halo[it, 2, d])
            o[d, :, 7] -= weight * (w[d, :, 7] - high_j * halo[it, 3, d])
        return go

    def boundary(it, spots):
        def go():
            left_h, left_l, right = [], [], []
            for dx, dz in spots:
                n = chip(-dx, -dz)
                left_h.append(mh[n])
                left_l.append(ml[n])
                right.append(xb[it, 2 * n])
                right.append(xb[it, 2 * n + 1])
            xh, xl = halves(jnp.concatenate(right, axis=0))
            part[...] += dot3(jnp.concatenate(left_h, axis=1), jnp.concatenate(left_l, axis=1), xh, xl)
        return go

    spots_of = [[] for _ in range(7)]
    for dx in (0, 1, -1, 2):
        for dz in (0, 1, -1, 2, -2, 3, -3, 4):
            spots_of[abs(dx) + abs(dz)].append((dx, dz))

    def gather(it, tasks, pops):
        tasks = list(tasks)
        xr = xb.at[it]

        def send(p, block, target):
            pltpu.make_async_remote_copy(
                src_ref=xr.at[block, PARTS[p]], dst_ref=xr.at[block, PARTS[p]],
                send_sem=gsend.at[it], recv_sem=grecv.at[it, p, block],
                device_id=(target, y), device_id_type=MESH,
            ).start()

        def wait(p, block):
            piece = xr.at[block, PARTS[p]]
            pltpu.make_async_copy(piece, piece, grecv.at[it, p, block]).wait()

        def share(block):
            pltpu.make_async_remote_copy(
                src_ref=xr.at[block], dst_ref=xr.at[block],
                send_sem=gsend.at[it], recv_sem=grecv.at[it, 0, block],
                device_id=(sibling, y), device_id_type=MESH,
            ).start()

        def shared(spots):
            def go():
                for dx, dz in spots:
                    block = at(-dx, -dz) + sgn
                    pltpu.make_async_copy(xr.at[block], xr.at[block], grecv.at[it, 0, block]).wait()
            return go

        def work(n):
            for _ in range(n):
                if tasks:
                    tasks.pop(0)()

        for p in (0, 1):
            for dx, dz in ((0, 1), (0, -1), (1, 0), (-1, 0)):
                send(p, s, at(dx, dz))
        share(s)
        part[...] = jnp.zeros_like(part)
        ready = list(spots_of[0])
        work(pops)
        for r in range(1, 7):
            for dx, dz in spots_of[r]:
                block = at(-dx, -dz)
                wait(0, block)
                if dz == 0:
                    send(0, block, at(0, 1))
                    send(0, block, at(0, -1))
                elif abs(dz) < 3 or (abs(dz) == 3 and (dx in (0, 1)) == (dz > 0)):
                    send(0, block, at(0, sign(dz)))
                wait(1, block)
                if dx == 0:
                    if abs(dz) < 3:
                        send(1, block, at(0, sign(dz)))
                    send(1, block, at(1, 0))
                    send(1, block, at(-1, 0))
                elif abs(dx) == 1 and (dz in (0, 1, -2, 3)) == (dx > 0):
                    send(1, block, at(sign(dx), 0))
                share(block)
                if (dx, dz) == (-1, 0):
                    send(0, at(-sgn, 0), at(sgn, 0))
                if (dx, dz) == (0, -3):
                    send(1, at(0, -3 * sgn), at(0, sgn))
                work(pops)
            ready += spots_of[r - 1] if r > 1 else []
            fresh = spots_of[r - 1]
            tasks.append(shared(fresh))
            while len(ready) >= 2:
                tasks.append(boundary(it, ready[:2]))
                ready = ready[2:]
        ready += spots_of[6]
        work(len(tasks))
        shared(spots_of[6])()
        boundary(it, ready)()

    def reduce(it):
        for i in range(1, GROUPS):
            other = (y + i) % GROUPS
            pltpu.make_async_remote_copy(
                src_ref=part.at[pl.ds(pl.multiple_of(FACE * other, FACE), FACE)], dst_ref=rsbuf.at[it, i - 1],
                send_sem=rsend.at[it], recv_sem=rrecv.at[it],
                device_id=(s, other), device_id_type=MESH,
            ).start()
        own = part[pl.ds(pl.multiple_of(FACE * y, FACE), FACE)]
        pltpu.make_async_copy(rsbuf.at[it], rsbuf.at[it], rrecv.at[it]).wait()
        total = own + rsbuf[it, 0] + rsbuf[it, 1] + rsbuf[it, 2]
        three = part.at[pl.ds(0, 3 * FACE)]
        pltpu.make_async_copy(three, three, rsend.at[it]).wait()
        return total

    lead.wait()
    rows_out(0, exact(node_out, u2[0]))
    rest.wait()
    rows_turn(0)
    xb[0, s] = exact(slot_in, rows_in(0))

    tasks = [get_m.wait] + [split_m(p) for p in range(16)]
    tasks += [face_out(0, u), get_k.wait] + [split_u(u2, d) for d in range(3)]
    tasks += [split_k(0, r) for r in range(4)] + [get_l.wait]
    tasks += [volume(u2, v2, 0, r) for r in range(2)]
    tasks += [face_in(0), faces(0, u, v, u2, v2, 0)]
    tasks += [lambda: rows_out(1, exact(node_out, v2[0]))]
    for d in (1, 2):
        tasks += [split_k(d, r) for r in range(4)] + [volume(u2, v2, d, r) for r in range(2)]
        tasks += [faces(0, u, v, u2, v2, d)]
    tasks += [lambda: rows_turn(1)]
    gather(0, tasks, 2)
    traction = reduce(0)
    xb[1, s] = exact(slot_in, rows_in(1)) - damping * traction
    tr[...] = traction

    def first_top():
        on_nodes = exact(node_in, rows_in(2))
        v2[0] -= damping * on_nodes
        pltpu.make_async_copy(halo.at[0], halo.at[0], hsend.at[0]).wait()

    tasks = [lambda: rows_out(2, exact(slot_out, tr[...])), lambda: None, lambda: rows_turn(2), lambda: None]
    tasks += [first_top, face_out(1, v)] + [split_u(v2, d) for d in range(3)]
    for d in (2, 1, 0):
        tasks += [volume(v2, u2, d, r) for r in range(2)]
    tasks += [face_in(1)] + [faces(1, v, u, v2, u2, d) for d in (2, 1, 0)]
    deep = pltpu.make_async_copy(u2.at[pl.ds(1, 2)], sol.at[pl.ds(1, 2)], osem.at[0])
    tasks += [deep.start]
    gather(1, tasks, 2)
    traction = reduce(1)
    tr[...] = traction
    rows_out(3, exact(slot_out, traction))
    put_tr = pltpu.make_async_copy(tr, trac, osem.at[1])
    put_tr.start()
    rows_turn(3)
    u2[0] -= damping * exact(node_in, rows_in(3))
    last = pltpu.make_async_copy(u2.at[0], sol.at[0], osem.at[2])
    last.start()

    for it in range(2):
        most = xb.at[it, pl.ds(0, 63)]
        pltpu.make_async_copy(most, most, gsend.at[it]).wait()
    pltpu.make_async_copy(halo.at[1], halo.at[1], hsend.at[1]).wait()
    for k in range(4):
        for phase in range(2):
            seven = abuf.at[k, :, pl.ds(0, 56)]
            pltpu.make_async_copy(seven, seven, asend.at[k, phase]).wait()
    deep.wait()
    put_tr.wait()
    last.wait()


def shards(stiffness, load, start, boundary_matrix, bem_node):
    nodes = bem_node.reshape(NX, NZ, NC, FACE)
    map_a = nodes.transpose(0, 2, 1, 3).reshape(FACE, FACE)
    map_b = nodes.transpose(3, 1, 0, 2).reshape(FACE, FACE)
    anywhere = pl.BlockSpec(memory_space=pl.ANY)
    vmem = pl.BlockSpec(memory_space=pltpu.VMEM)
    dma = pltpu.SemaphoreType.DMA
    field = (DEPTH, EDGE, EDGE, EDGE, FIELDS)
    flat = (DEPTH, NODES, FIELDS)
    sol, trac = pl.pallas_call(
        kernel,
        out_shape=(
            jax.ShapeDtypeStruct(flat, F32),
            jax.ShapeDtypeStruct((FACE, FIELDS), F32),
        ),
        in_specs=[anywhere] * 4 + [vmem] * 2,
        out_specs=(anywhere, anywhere),
        scratch_shapes=[
            pltpu.VMEM(field, F32), pltpu.VMEM(field, F32), pltpu.VMEM(flat, F32),
            pltpu.VMEM(flat, BF16), pltpu.VMEM(flat, BF16),
            pltpu.VMEM((DEPTH, NODES, NODES), F32),
            pltpu.VMEM((DEPTH, NODES, NODES), BF16), pltpu.VMEM((DEPTH, NODES, NODES), BF16),
            pltpu.VMEM((FACE, GROUPS, COLS), F32),
            pltpu.VMEM((32, 256, 128), BF16), pltpu.VMEM((32, 256, 128), BF16),
            pltpu.VMEM((2, 64, FACE, FIELDS), F32),
            pltpu.VMEM((256, FIELDS), F32),
            pltpu.VMEM((2, 3, FACE, FIELDS), F32),
            pltpu.VMEM((2, 4, DEPTH, EDGE, EDGE, FIELDS), F32),
            pltpu.VMEM((FACE, FIELDS), F32),
            *[pltpu.VMEM((4, 2, FACE, 128), F32)] * 4,
            dma((5,)), dma((2,)), dma((2, 2, 64)), dma((4, 2)), dma((4, 2)),
            dma((2,)), dma((2,)), dma((2,)), dma((2,)), dma((3,)),
        ],
        compiler_params=pltpu.CompilerParams(
            collective_id=0, has_side_effects=True, vmem_limit_bytes=58 * 2**20
        ),
        name="interface_iterations",
    )(stiffness[0], load[0], start[0], boundary_matrix, map_a, map_b)
    return sol[None], trac[None]


def solution(mesh):
    in_specs = (
        P(("surf", "col"), None, None, None),
        P(("surf", "col"), None, None, None),
        P(("surf", "col"), None, None, None),
        P("surf", None, "col"),
        P("col", None),
    )
    out_specs = (P(("surf", "col"), None, None, None), P("col", "surf", None))
    return jax.shard_map(shards, mesh=mesh, in_specs=in_specs, out_specs=out_specs, check_vma=False)
```

time: 463 us -> 117 us (0.25)
  waiting for transfers between devices: 250 us -> 0 us
  Pallas kernels: 0 us -> 110 us
  local copies, waits for them, and re-layouts: 110 us -> 5.24 us
  other arithmetic: 38.9 us -> 1.4 us
  matrix products: 25.3 us -> 0 us
  starting transfers between devices: 23.2 us -> 0 us
  between operations: 14.4 us -> 0.66 us
    all_gather x4 -> x0, waiting for transfers between devices: 200 us -> none  [the longest x2 157 us: shards(): gathered = lax.all_gather(top_face, 'surf', axis=0, tiled=True)]
    pallas_call x0 -> x1, Pallas kernels: none -> 110 us  [shards(): pl.pallas_call(kernel, out_shape=(jax.ShapeDtypeStruct(flat, F32), jax.Sh...]
    gather x4 -> x0, local copies, waits for them, and re-layouts: 42.3 us -> none  [the longest x2 36.6 us: shards(): ordered = jnp.take(gathered, group_map, axis=0)]
    scatter-add x12 -> x0, local copies, waits for them, and re-layouts: 40.4 us -> none  [the longest x2 9 us: volume_apply(): extra = extra.at[:, :, 0].add(cube[:, :, 0] - padded[:, 1:-1, 0])]
    reduce_scatter x2 -> x0, waiting for transfers between devices: 35.9 us -> none  [shards(): lax.psum_scatter(partial_value.reshape(face_nodes, -1, fields), 'col', sc...]
    add x12 -> x0, other arithmetic: 27.8 us -> none  [the longest x2 6.89 us: volume_apply(): return applied.reshape(cube.shape) + coupling * extra]
    dot_general x4 -> x0, matrix products: 25.3 us -> none  [the longest x2 14.7 us: shards(): jnp.dot(operator_rows, ordered, precision=highest, preferred_element_type...]
    ppermute x8 -> x0, starting transfers between devices: 23 us -> none  [the longest x4 16.4 us: with_halo(): lax.ppermute(lax.slice_in_dim(block, block.shape[dim] - width, None, axis...]
  transfers between devices with their start and end apart: 14 -> 0, of which waited for: 10 -> 0; matrix products, arithmetic and copies ran while one was open for 21% -> 0% of each run, Pallas kernels for 0% -> 0%
where the time goes in v1:
time: 117 us
  Pallas kernels  110 us (94%)
  local copies, waits for them, and re-layouts  5.24 us (4%)
  other arithmetic  1.4 us (1%)
    pallas_call x1, Pallas kernels, shards(): pl.pallas_call(kernel, out_shape=(jax.ShapeDtypeStruct(flat, F32), jax.Sh...  110 us
    unnamed x5, local copies, waits for them, and re-layouts  3.83 us

profile of v1, /device:TPU:1, one launch (start us, length us, event | category | flops | bytes accessed | tf_op | source)
XLA Modules:
  0.0 116.9 jit_solution(5484166859497659569)
XLA Ops:
  0.6 0.5 broadcast.3
  1.1 1.4 %reduce.3 = s32[4096]{0:T(1024)S(1)} reduce(s32[1,4096]{1,0:T(1,128)} %param.9, s32[]{:T(128)} %broadcast.3), dimensions={0}, to_apply=%param.9.reduce_sub_computation.3 | reduce | bytes 32772 | tf_op args[4]
  2.5 0.1 reshape.13
  2.7 0.6 copy.9
  3.3 0.7 copy.11.map_b
  4.0 109.6 %interface_iterations.1 = (f32[3,512,256]{2,1,0:T(8,128)}, f32[64,256]{1,0:T(8,128)}) custom-call(f32[3,512,512]{2,1,0:T(8,128)} %bitcast.11, f32[3,512,256]{2,1,0:T(8,128)} %bitcast.12, f32[3,512,256]{2,1,0:T(8,128)} %bitcast.13, f32[64,4,4096]{2,1,0:T(4,128)} %bm.1, s32[64,64]{1,0:T(8,128)} %bitcast.15, s32[64,64]{1,0:T(8,128)} %copy.11.map_b), custom_call_target="tpu_custom_call" | custom-call | tf_op jit(solution)/shard_map/interface_iterations/pallas_call | solution.py:385
  113.6 0.0 copy-start
  113.6 2.7 %copy.14 = f32[1,3,512,256]{3,2,1,0:T(8,128)} copy(f32[1,3,512,256]{3,2,1,0:T(8,128)} %bitcast.14) | data formatting | bytes 3145728
  116.3 0.0 copy-done
  116.3 0.6 copy.15
  (1 shorter events, 0.0 us)
Async XLA Ops:
  113.6 2.7 %copy-start = (f32[64,256]{1,0:T(8,128)S(1)}, f32[64,256]{1,0:T(8,128)}, u32[]{:S(2)}) copy-start(f32[64,256]{1,0:T(8,128)} %get-tuple-element.5) | copy-start | bytes 196612

commit v2 on v1

v2 whole, which is shorter than its diff:
```python
import functools

import jax
import jax.numpy as jnp
from jax import lax
from jax.experimental import pallas as pl
from jax.experimental.pallas import tpu as pltpu
from jax.sharding import PartitionSpec as P

MESH = pl.DeviceIdType.MESH
F32, BF16 = jnp.float32, jnp.bfloat16
LAG = 8
NX, NZ, NC = 4, 8, 2
EDGE, DEPTH, NODES, FACE, FIELDS = 8, 3, 512, 64, 256
GROUPS, COLS = 4, 4096
SPLIT = 24
PARTS = (pl.ds(0, SPLIT), pl.ds(SPLIT, FACE - SPLIT))
damping = 0.25
coupling = 0.5


FIRST = (
    (0, 0, 1), (1, 0, -2), (1, 0, -1), (1, 0, 2), (0, 1, 0), (1, 0, 1), (0, 0, -2), (1, -1, 0), (0, -1, 0), (1, 1, 0),
)
ARRIVALS = (
    (0, 1, 0, ((0, -1), (1, 0))), (0, 0, 1, ((0, 2), (1, 0), (-1, 0))),
    (1, -1, 0, ((0, 1), (-1, 0))), (1, 1, 0, ()),
    (0, -1, 0, ()), (1, 0, -2, ((0, -1), (0, -2), (1, 0))),
    (1, 0, 2, ((-1, 0), (1, 0))), (1, 0, -1, ((-1, 0), (1, 0))),
    (1, 0, 1, ((1, 0),)), (0, 2, 0, ((0, 1),)),
    (0, -1, 1, ((0, 1),)), (0, 0, -2, ((0, -1), (1, 0), (0, 1), (-1, 0))),
    (0, 1, 1, ((0, 1),)), (0, 1, -1, ((1, 0),)),
    (0, 0, 3, ((-1, 0), (0, 1))), (1, 2, 0, ()),
    (1, 1, -2, ()), (1, 0, -3, ((-1, 0), (1, 0))),
    (1, -1, 1, ()), (1, -1, 2, ((-1, 0),)),
    (1, 1, 2, ((0, 1),)), (1, -1, -1, ((-1, 0),)),
    (1, 0, 4, ((0, -1), (1, 0))), (1, 1, -1, ()),
    (0, -1, -2, ()), (0, -1, 3, ((-1, 0), (0, 1))),
    (1, 1, 1, ((1, 0),)), (0, 2, 1, ()),
    (0, 1, -2, ((0, -1), (1, 0))), (0, -1, 2, ()),
    (1, -1, -3, ((0, 1), (0, -1), (-1, 0))), (0, 2, -1, ((1, 0), (0, -2))),
    (0, 0, -1, ()), (1, 2, 2, ((0, 1),)),
    (1, 1, -3, ()), (0, 1, 2, ((-1, 0), (0, 1), (1, 0))),
    (0, 0, -3, ((-1, 0),)), (0, 0, 4, ((1, 0),)),
    (1, 2, -1, ((0, -1),)), (1, 1, 4, ((1, 0),)),
    (1, 0, 3, ((-1, 0),)), (0, 2, 3, ((0, 1),)),
    (1, 1, 3, ()), (1, 2, 1, ()),
    (0, 1, -3, ()), (0, -1, 4, ()),
    (0, 2, -2, ()), (1, 2, -3, ()),
    (1, -1, 4, ()), (0, -1, -1, ()),
    (1, -1, -2, ()), (0, 0, 2, ()),
    (0, 2, 2, ()), (0, -1, -3, ()),
    (1, 2, 3, ()), (0, 2, -3, ()),
    (0, 1, 4, ()), (0, 1, 3, ()),
    (1, -1, 3, ()), (1, 2, -2, ()),
    (1, 2, 4, ()), (0, 2, 4, ()),
)


def halves(a):
    high = a.astype(BF16)
    return high, (a - high.astype(F32)).astype(BF16)


def dot(a, b):
    return jnp.dot(a, b, preferred_element_type=F32)


def dot_t(a, b):
    return lax.dot_general(a, b, (((1,), (1,)), ((), ())), preferred_element_type=F32)


def dot3(ah, al, bh, bl):
    return dot(ah, bh) + dot(al, bh) + dot(ah, bl)


def exact(onehot, rows):
    high, low = halves(rows)
    least = (rows - high.astype(F32) - low.astype(F32)).astype(BF16)
    return dot(onehot, high) + dot(onehot, low) + dot(onehot, least)


def kernel(
    stiff, load, start, bm, nodes, sol, trac,
    u, v, ld, uh, ul, kraw, kh, kl, mraw, mh, ml, nh, nl, xb, part, rsbuf, halo, tr,
    asrc, abuf, bsrc, bbuf,
    lsem, gsend, grecv, asend, arecv, rsend, rrecv, hsend, hrecv, osem,
):
    s, y = lax.axis_index("surf"), lax.axis_index("col")
    c, z, x = s % NC, (s // NC) % NZ, s // (NC * NZ)
    sgn = 1 - 2 * c
    xc = c * NX + x
    u2, v2 = u.reshape(DEPTH, NODES, FIELDS), v.reshape(DEPTH, NODES, FIELDS)

    def at(dx, dz):
        return ((x + NX + dx) % NX * NZ + (z + NZ + dz) % NZ) * NC + c

    def chip(dx, dz):
        return (x + NX + dx) % NX * NZ + (z + NZ + dz) % NZ

    sibling = s + sgn
    up, down = (s + 1) % (NX * NZ * NC), (s + NX * NZ * NC - 1) % (NX * NZ * NC)

    def mate_xc(i):
        other = (xc + i) % (NX * NC)
        return other, (other % NX * NZ + z) * NC + other // NX

    def mate_z(i):
        other = (z + i) % NZ
        return other, (x * NZ + other) * NC + c

    lead = pltpu.make_async_copy(start.at[0], u2.at[0], lsem.at[0])
    rest = pltpu.make_async_copy(start.at[pl.ds(1, 2)], u2.at[pl.ds(1, 2)], lsem.at[1])
    get_m = [pltpu.make_async_copy(bm.at[:, g], mraw.at[g], lsem.at[5 + g]) for g in range(GROUPS)]
    get_k = pltpu.make_async_copy(stiff, kraw, lsem.at[3])
    get_l = pltpu.make_async_copy(load, ld, lsem.at[4])
    for copy in (lead, *get_m, rest, get_k, get_l):
        copy.start()

    barrier = pltpu.get_barrier_semaphore()

    def greet(surf, col):
        pl.semaphore_signal(barrier, inc=1, device_id=(surf, col), device_id_type=MESH)

    for i in range(1, NX * NC):
        greet(mate_xc(i)[1], y)
    for i in range(1, NZ):
        greet(mate_z(i)[1], y)
    for i in range(1, GROUPS):
        greet(s, (y + i) % GROUPS)
    greet((s + NX * NZ * NC - sgn) % (NX * NZ * NC), y)
    pl.semaphore_wait(barrier, NX * NC - 1 + NZ - 1 + GROUPS - 1 + 1)

    sub = lax.broadcasted_iota(jnp.int32, (FACE, FACE), 0)
    lane = lax.broadcasted_iota(jnp.int32, (FACE, FACE), 1)
    pairs = nodes[...]
    held = jnp.concatenate([pairs[:, :FACE], pairs[:, FACE:]], axis=0)
    mine = jnp.sum(jnp.where((held >> 6) == s, held & 63, 0), axis=1, keepdims=True)
    lane_8 = lax.broadcasted_iota(jnp.int32, (FACE, NODES), 1)
    node_out = (mine * EDGE == lane_8).astype(F32).astype(BF16)
    turned = jnp.sum(jnp.where(sub == (lane & 7) * 8 + (lane >> 3), mine, 0), axis=0, keepdims=True)
    sub_8 = lax.broadcasted_iota(jnp.int32, (NODES, FACE), 0)
    node_in = (turned * EDGE == sub_8).astype(F32).astype(BF16)
    patch = jnp.sum(jnp.where(sub == xc * NZ + z, held, 0), axis=0, keepdims=True) >> 6
    slot_out = ((patch & 1) * 32 + (patch >> 1) == sub).astype(F32).astype(BF16)
    column = jnp.sum(jnp.where(sub == lane, patch, 0), axis=1, keepdims=True)
    slot_in = (((column >> 1) & 7) * 8 + (column & 1) * NX + (column >> 4) == lane).astype(F32).astype(BF16)

    def eight(i):
        return pl.ds(pl.multiple_of(i * 8, 8), 8)

    def rows_out(k, rows):
        for h in range(2):
            asrc[k, h] = rows[:, 128 * h : 128 * h + 128]
        abuf[k, :, eight(xc)] = asrc[k, :, eight(xc)]
        for i in range(1, NX * NC):
            other, target = mate_xc(i)
            pltpu.make_async_remote_copy(
                src_ref=asrc.at[k, :, eight(other)], dst_ref=abuf.at[k, :, eight(xc)],
                send_sem=asend.at[k, 0], recv_sem=arecv.at[k, 0],
                device_id=(target, y), device_id_type=MESH,
            ).start()

    def rows_turn(k):
        seven = abuf.at[k, :, pl.ds(0, 56)]
        pltpu.make_async_copy(seven, seven, arecv.at[k, 0]).wait()
        for h in range(2):
            for i in range(NZ):
                bsrc[k, h, pl.ds(8 * i, 8)] = abuf[k, h, pl.ds(i, 8, stride=8)]
        bbuf[k, :, eight(z)] = bsrc[k, :, eight(z)]
        for i in range(1, NZ):
            other, target = mate_z(i)
            pltpu.make_async_remote_copy(
                src_ref=bsrc.at[k, :, eight(other)], dst_ref=bbuf.at[k, :, eight(z)],
                send_sem=asend.at[k, 1], recv_sem=arecv.at[k, 1],
                device_id=(target, y), device_id_type=MESH,
            ).start()

    def rows_in(k):
        seven = bbuf.at[k, :, pl.ds(0, 56)]
        pltpu.make_async_copy(seven, seven, arecv.at[k, 1]).wait()
        return jnp.concatenate([bbuf[k, 0], bbuf[k, 1]], axis=1)

    big_sub = lax.broadcasted_iota(jnp.int32, (128, 128), 0)
    big_lane = lax.broadcasted_iota(jnp.int32, (128, 128), 1)

    def split_m(p):
        def go():
            for n in (2 * p, 2 * p + 1):
                for g in range(GROUPS):
                    tile = mraw[g, :, pl.ds(128 * n, 128)]
                    mh[n, pl.ds(FACE * g, FACE)], ml[n, pl.ds(FACE * g, FACE)] = halves(tile)
        return go

    named = dot_t((big_sub == big_lane).astype(F32).astype(BF16), (pairs >> 6).astype(F32).astype(BF16))
    wide_sub = lax.broadcasted_iota(jnp.int32, (256, 256), 0)
    wide_lane = lax.broadcasted_iota(jnp.int32, (256, 256), 1)
    wanted = jnp.where((wide_sub >> 6) == (wide_lane >> 6), wide_lane & 63, -1).astype(F32)

    def order_m(n):
        def go():
            row = jnp.concatenate([named[:, 2 * n : 2 * n + 1], named[:, 2 * n + 1 : 2 * n + 2]], axis=0)
            place = jnp.where(row == wanted, 1.0, 0.0).astype(BF16)
            nh[n] = dot(jnp.concatenate([mh[2 * n], mh[2 * n + 1]], axis=1), place).astype(BF16)
            nl[n] = dot(jnp.concatenate([ml[2 * n], ml[2 * n + 1]], axis=1), place).astype(BF16)
        return go

    def split_k(d, r):
        def go():
            kh[d, pl.ds(128 * r, 128)], kl[d, pl.ds(128 * r, 128)] = halves(kraw[d, pl.ds(128 * r, 128)])
        return go

    def split_u(w2, d):
        def go():
            uh[d], ul[d] = halves(w2[d])
        return go

    def face_out(it, w):
        def go():
            for k, (src, target) in enumerate((
                (w.at[:, 7], (up, y)),
                (w.at[:, 0], (down, y)),
                (w.at[:, :, 7], (s, (y + 1) % GROUPS)),
                (w.at[:, :, 0], (s, (y + GROUPS - 1) % GROUPS)),
            )):
                pltpu.make_async_remote_copy(
                    src_ref=src, dst_ref=halo.at[it, k], send_sem=hsend.at[it], recv_sem=hrecv.at[it],
                    device_id=target, device_id_type=MESH,
                ).start()
        return go

    def face_in(it):
        def go():
            pltpu.make_async_copy(halo.at[it], halo.at[it], hrecv.at[it]).wait()
        return go

    low_i = jnp.where(s > 0, 1.0, 0.0).astype(F32)
    high_i = jnp.where(s < NX * NZ * NC - 1, 1.0, 0.0).astype(F32)
    low_j = jnp.where(y > 0, 1.0, 0.0).astype(F32)
    high_j = jnp.where(y < GROUPS - 1, 1.0, 0.0).astype(F32)
    weight = damping * coupling

    layer = lax.broadcasted_iota(jnp.int32, (32, EDGE, FIELDS), 1)

    def volume(w2, o2, d, r):
        def go():
            block = pl.ds(256 * r, 256)
            applied = dot3(kh[d, block], kl[d, block], uh[d], ul[d])
            here = w2[d, block].reshape(32, EDGE, FIELDS)
            term = here
            if d + 1 < DEPTH:
                term = here - pltpu.roll(w2[d + 1, block].reshape(32, EDGE, FIELDS), 7, 1)
            term = jnp.where(layer == EDGE - 1, term, 0.0)
            if d:
                above = here - pltpu.roll(w2[d - 1, block].reshape(32, EDGE, FIELDS), 1, 1)
                term = jnp.where(layer == 0, above, term)
            out = w2[d, block] + damping * (ld[d, block] - applied)
            o2[d, block] = out - weight * term.reshape(256, FIELDS)
        return go

    def faces(it, w, o, w2, o2, d):
        def go():
            o[d, 0] -= weight * (w[d, 0] - low_i * halo[it, 0, d])
            o[d, 7] -= weight * (w[d, 7] - high_i * halo[it, 1, d])
            o[d, :, 0] -= weight * (w[d, :, 0] - low_j * halo[it, 2, d])
            o[d, :, 7] -= weight * (w[d, :, 7] - high_j * halo[it, 3, d])
        return go

    x2 = xb.reshape(2, 2, 64 * FACE, 128)

    def boundary(it, spots):
        def go():
            left_h, left_l, right = [], [], []
            for dx, dz in spots:
                n = chip(-dx, -dz)
                left_h.append(mh[n])
                left_l.append(ml[n])
                rows = pl.ds(pl.multiple_of(128 * n, 128), 128)
                right.append(jnp.concatenate([x2[it, 0, rows], x2[it, 1, rows]], axis=1))
            xh, xl = halves(jnp.concatenate(right, axis=0))
            part[...] += dot3(jnp.concatenate(left_h, axis=1), jnp.concatenate(left_l, axis=1), xh, xl)
        return go

    def boundary_by_node(n):
        right = []
        for block in range(2 * n, 2 * n + 4):
            rows = pl.ds(block % 2 * 32 + block // 2, FACE, stride=FACE)
            right.append(jnp.concatenate([x2[0, 0, rows], x2[0, 1, rows]], axis=1))
        xh, xl = halves(jnp.concatenate(right, axis=0))
        part[...] += dot3(nh[n // 2], nl[n // 2], xh, xl)

    def put_x(it, rows):
        for h in range(2):
            xb[it, h, s] = rows[:, 128 * h : 128 * h + 128]

    def gather(it, tasks, pops):
        tasks = list(tasks)
        xr = xb.at[it]

        def send(p, block, target):
            pltpu.make_async_remote_copy(
                src_ref=xr.at[:, block, PARTS[p]], dst_ref=xr.at[:, block, PARTS[p]],
                send_sem=gsend.at[it], recv_sem=grecv.at[it, p, block],
                device_id=(target, y), device_id_type=MESH,
            ).start()

        def wait(p, block):
            piece = xr.at[:, block, PARTS[p]]
            pltpu.make_async_copy(piece, piece, grecv.at[it, p, block]).wait()

        def share(block):
            pltpu.make_async_remote_copy(
                src_ref=xr.at[:, block], dst_ref=xr.at[:, block],
                send_sem=gsend.at[it], recv_sem=grecv.at[it, 0, block],
                device_id=(sibling, y), device_id_type=MESH,
            ).start()

        def shared(spots):
            def go():
                for dx, dz in spots:
                    block = at(-dx, -dz) + sgn
                    pltpu.make_async_copy(xr.at[:, block], xr.at[:, block], grecv.at[it, 0, block]).wait()
            return go

        def work(now, most):
            while tasks and tasks[0][0] <= now and most:
                tasks.pop(0)[1]()
                most -= 1

        for p, dx, dz in FIRST:
            send(p, s, at(dx, dz))
        share(s)
        part[...] = jnp.zeros_like(part)
        work(-1, pops)
        seen, fresh = {(0, 0): 2}, [(0, 0)]
        for now, (p, dx, dz, onward) in enumerate(ARRIVALS):
            block = at(-dx, -dz)
            wait(p, block)
            for tx, tz in onward:
                send(p, block, at(tx, tz))
            seen[dx, dz] = seen.get((dx, dz), 0) + 1
            if seen[dx, dz] == 2:
                share(block)
                fresh.append((dx, dz))
            if it and now >= 12 and len(fresh) > LAG:
                early, fresh = fresh[:2], fresh[2:]
                tasks[:0] = [(0, shared(early)), (0, boundary(it, early))]
            work(now, pops)
        work(99, 99)
        shared(fresh)()
        if it:
            for i in range(0, len(fresh), 4):
                boundary(it, fresh[i : i + 4])()
        else:
            for n in range(0, 32, 2):
                boundary_by_node(n)

    def reduce(it, tasks):
        for i in (2, 1, 3):
            other = (y + i) % GROUPS
            pltpu.make_async_remote_copy(
                src_ref=part.at[pl.ds(pl.multiple_of(FACE * other, FACE), FACE)], dst_ref=rsbuf.at[it, i - 1],
                send_sem=rsend.at[it], recv_sem=rrecv.at[it],
                device_id=(s, other), device_id_type=MESH,
            ).start()
        for task in tasks:
            task()
        own = part[pl.ds(pl.multiple_of(FACE * y, FACE), FACE)]
        pltpu.make_async_copy(rsbuf.at[it], rsbuf.at[it], rrecv.at[it]).wait()
        total = own + rsbuf[it, 0] + rsbuf[it, 1] + rsbuf[it, 2]
        three = part.at[pl.ds(0, 3 * FACE)]
        pltpu.make_async_copy(three, three, rsend.at[it]).wait()
        return total

    lead.wait()
    put_x(0, exact(node_out, u2[0]))
    early = [rest.wait] + [copy.wait for copy in get_m] + [split_m(p) for p in range(16)] + [order_m(n) for n in range(16)]
    later = [get_k.wait] + [split_u(u2, d) for d in range(3)]
    later += [split_k(0, r) for r in range(4)] + [get_l.wait] + [volume(u2, v2, 0, r) for r in range(2)]
    tasks = [(-1, task) for task in early[:13]] + [(0, task) for task in early[13:]]
    tasks[13:13] = [(3, face_out(0, u))]
    tasks += [(0, task) for task in later]
    tasks += [(36, face_in(0)), (36, faces(0, u, v, u2, v2, 0))]
    tasks += [(36, lambda: rows_out(1, exact(node_out, v2[0])))]
    for d in (1, 2):
        tasks += [(0, split_k(d, r)) for r in range(4)] + [(0, volume(u2, v2, d, r)) for r in range(2)]
        tasks += [(0, faces(0, u, v, u2, v2, d))]
    tasks += [(56, lambda: rows_turn(1))]
    gather(0, tasks, 3)
    traction = reduce(0, [])
    put_x(1, exact(slot_in, rows_in(1)) - damping * traction)
    tr[...] = traction

    def first_top():
        v2[0] -= damping * exact(node_in, rows_in(2))
        pltpu.make_async_copy(halo.at[0], halo.at[0], hsend.at[0]).wait()

    tasks = [(-1, lambda: rows_out(2, exact(slot_out, tr[...]))), (14, lambda: rows_turn(2))]
    tasks += [(30, first_top), (30, face_out(1, v))] + [(30, split_u(v2, d)) for d in range(3)]
    for d in (2, 1, 0):
        tasks += [(0, volume(v2, u2, d, r)) for r in range(2)]
    gather(1, tasks, 3)
    deep = pltpu.make_async_copy(u2.at[pl.ds(1, 2)], sol.at[pl.ds(1, 2)], osem.at[0])
    traction = reduce(1, [face_in(1)] + [faces(1, v, u, v2, u2, d) for d in (2, 1, 0)] + [deep.start])
    tr[...] = traction
    rows_out(3, exact(slot_out, traction))
    put_tr = pltpu.make_async_copy(tr, trac, osem.at[1])
    put_tr.start()
    rows_turn(3)
    u2[0] -= damping * exact(node_in, rows_in(3))
    last = pltpu.make_async_copy(u2.at[0], sol.at[0], osem.at[2])
    last.start()

    for it in range(2):
        most = xb.at[it, :, pl.ds(0, 63)]
        pltpu.make_async_copy(most, most, gsend.at[it]).wait()
    pltpu.make_async_copy(halo.at[1], halo.at[1], hsend.at[1]).wait()
    for k in (1, 2, 3):
        for phase in range(2):
            seven = abuf.at[k, :, pl.ds(0, 56)]
            pltpu.make_async_copy(seven, seven, asend.at[k, phase]).wait()
    deep.wait()
    put_tr.wait()
    last.wait()


def shards(stiffness, load, start, boundary_matrix, bem_node):
    anywhere = pl.BlockSpec(memory_space=pl.ANY)
    vmem = pl.BlockSpec(memory_space=pltpu.VMEM)
    dma = pltpu.SemaphoreType.DMA
    field = (DEPTH, EDGE, EDGE, EDGE, FIELDS)
    flat = (DEPTH, NODES, FIELDS)
    sol, trac = pl.pallas_call(
        kernel,
        out_shape=(
            jax.ShapeDtypeStruct(flat, F32),
            jax.ShapeDtypeStruct((FACE, FIELDS), F32),
        ),
        in_specs=[anywhere] * 4 + [vmem],
        out_specs=(anywhere, anywhere),
        scratch_shapes=[
            pltpu.VMEM(field, F32), pltpu.VMEM(field, F32), pltpu.VMEM(flat, F32),
            pltpu.VMEM(flat, BF16), pltpu.VMEM(flat, BF16),
            pltpu.VMEM((DEPTH, NODES, NODES), F32),
            pltpu.VMEM((DEPTH, NODES, NODES), BF16), pltpu.VMEM((DEPTH, NODES, NODES), BF16),
            pltpu.VMEM((GROUPS, FACE, COLS), F32),
            *[pltpu.VMEM((32, 256, 128), BF16)] * 2,
            *[pltpu.VMEM((16, 256, 256), BF16)] * 2,
            pltpu.VMEM((2, 2, 64, FACE, 128), F32),
            pltpu.VMEM((256, FIELDS), F32),
            pltpu.VMEM((2, 3, FACE, FIELDS), F32),
            pltpu.VMEM((2, 4, DEPTH, EDGE, EDGE, FIELDS), F32),
            pltpu.VMEM((FACE, FIELDS), F32),
            *[pltpu.VMEM((4, 2, FACE, 128), F32)] * 4,
            dma((9,)), dma((2,)), dma((2, 2, 64)), dma((4, 2)), dma((4, 2)),
            dma((2,)), dma((2,)), dma((2,)), dma((2,)), dma((3,)),
        ],
        compiler_params=pltpu.CompilerParams(
            collective_id=0, has_side_effects=True, vmem_limit_bytes=58 * 2**20
        ),
        name="interface_iterations",
    )(stiffness[0], load[0], start[0], boundary_matrix, bem_node.reshape(32, 128))
    return sol[None], trac[None]


def solution(mesh):
    in_specs = (
        P(("surf", "col"), None, None, None),
        P(("surf", "col"), None, None, None),
        P(("surf", "col"), None, None, None),
        P("surf", None, "col"),
        P("col", None),
    )
    out_specs = (P(("surf", "col"), None, None, None), P("col", "surf", None))
    return jax.shard_map(shards, mesh=mesh, in_specs=in_specs, out_specs=out_specs, check_vma=False)
```

time: 117 us -> 89 us (0.76)
  Pallas kernels: 110 us -> 84.9 us
  local copies, waits for them, and re-layouts: 5.24 us -> 3.32 us
  other arithmetic: 1.4 us -> 0 us
    pallas_call x1, Pallas kernels: 110 us -> 84.9 us  [shards(): pl.pallas_call(kernel, out_shape=(jax.ShapeDtypeStruct(flat, F32), jax.Sh...]
    reshape x4 -> x0, local copies, waits for them, and re-layouts: 1.41 us -> none  [the longest x3 0.72 us: shards(): nodes = bem_node.reshape(NX, NZ, NC, FACE)]
    unnamed x1 -> x0, other arithmetic: 1.4 us -> none
    unnamed x5 -> x4, local copies, waits for them, and re-layouts: 3.83 us -> 3.32 us
where the time goes in v2:
time: 89 us; the launch traced here: 88.9 us
  Pallas kernels  84.9 us (95%)
  local copies, waits for them, and re-layouts  3.32 us (4%)
    pallas_call x1, Pallas kernels, shards(): pl.pallas_call(kernel, out_shape=(jax.ShapeDtypeStruct(flat, F32), jax.Sh...  84.9 us
    unnamed x4, local copies, waits for them, and re-layouts  3.32 us

profile of v2, /device:TPU:1, one launch (start us, length us, event | category | flops | bytes accessed | tf_op | source)
XLA Modules:
  0.0 88.9 jit_solution(15602295689310165311)
XLA Ops:
  0.6 84.9 %interface_iterations.1 = (f32[3,512,256]{2,1,0:T(8,128)}, f32[64,256]{1,0:T(8,128)}) custom-call(f32[3,512,512]{2,1,0:T(8,128)} %bitcast.6, f32[3,512,256]{2,1,0:T(8,128)} %bitcast.7, f32[3,512,256]{2,1,0:T(8,128)} %bitcast.8, f32[64,4,4096]{2,1,0:T(4,128)} %bm.1, s32[32,128]{1,0:T(8,128)} %bitcast.11), custom_call_target="tpu_custom_call" | custom-call | tf_op jit(solution)/shard_map/interface_iterations/pallas_call | solution.py:433
  85.6 0.0 copy-start
  85.6 2.7 %copy.9 = f32[1,3,512,256]{3,2,1,0:T(8,128)} copy(f32[1,3,512,256]{3,2,1,0:T(8,128)} %bitcast.9) | data formatting | bytes 3145728
  88.3 0.0 copy-done
  88.3 0.6 copy.10
Async XLA Ops:
  85.6 2.7 %copy-start = (f32[64,256]{1,0:T(8,128)S(1)}, f32[64,256]{1,0:T(8,128)}, u32[]{:S(2)}) copy-start(f32[64,256]{1,0:T(8,128)} %get-tuple-element.5) | copy-start | bytes 196612

commit v3 on v2

--- a/solution.py
+++ b/solution.py
@@ -9,6 +9,7 @@
 
 MESH = pl.DeviceIdType.MESH
 F32, BF16 = jnp.float32, jnp.bfloat16
+START = (30, 12)
 LAG = 8
 NX, NZ, NC = 4, 8, 2
 EDGE, DEPTH, NODES, FACE, FIELDS = 8, 3, 512, 64, 256
@@ -82,7 +83,7 @@
 
 def kernel(
     stiff, load, start, bm, nodes, sol, trac,
-    u, v, ld, uh, ul, kraw, kh, kl, mraw, mh, ml, nh, nl, xb, part, rsbuf, halo, tr,
+    u, v, ld, uh, ul, kraw, kh, kl, mraw, mh, ml, nh, nl, turned_m, xb, part, rsbuf, halo, tr,
     asrc, abuf, bsrc, bbuf,
     lsem, gsend, grecv, asend, arecv, rsend, rrecv, hsend, hrecv, osem,
 ):
@@ -192,17 +193,29 @@
                     mh[n, pl.ds(FACE * g, FACE)], ml[n, pl.ds(FACE * g, FACE)] = halves(tile)
         return go
 
-    named = dot_t((big_sub == big_lane).astype(F32).astype(BF16), (pairs >> 6).astype(F32).astype(BF16))
-    wide_sub = lax.broadcasted_iota(jnp.int32, (256, 256), 0)
-    wide_lane = lax.broadcasted_iota(jnp.int32, (256, 256), 1)
-    wanted = jnp.where((wide_sub >> 6) == (wide_lane >> 6), wide_lane & 63, -1).astype(F32)
+    def turn_m(n):
+        def go():
+            same = (big_sub >> 6) == (big_lane >> 6)
+            place = jnp.where(same & ((pairs[n : n + 1] >> 6) == (big_sub & 63)), 1.0, 0.0).astype(BF16)
+            rows = dot_t(place, mh[n]) + dot_t(place, ml[n])
+            for q in range(2):
+                turned_m[q, pl.ds(128 * n, 128)] = rows[:, 128 * q : 128 * q + 128]
+        return go
+
+    equal = (
+        lax.broadcasted_iota(jnp.int32, (256, 256), 0) == lax.broadcasted_iota(jnp.int32, (256, 256), 1)
+    ).astype(F32).astype(BF16)
 
     def order_m(n):
         def go():
-            row = jnp.concatenate([named[:, 2 * n : 2 * n + 1], named[:, 2 * n + 1 : 2 * n + 2]], axis=0)
-            place = jnp.where(row == wanted, 1.0, 0.0).astype(BF16)
-            nh[n] = dot(jnp.concatenate([mh[2 * n], mh[2 * n + 1]], axis=1), place).astype(BF16)
-            nl[n] = dot(jnp.concatenate([ml[2 * n], ml[2 * n + 1]], axis=1), place).astype(BF16)
+            slab = []
+            for q in range(2):
+                slab.append(jnp.concatenate([
+                    turned_m[q, pl.ds(core * FACE + 2 * n + k, 32, stride=128)] for k in range(2) for core in range(2)
+                ], axis=0))
+            high, low = halves(jnp.concatenate(slab, axis=1))
+            nh[n] = dot_t(equal, high).astype(BF16)
+            nl[n] = dot_t(equal, low).astype(BF16)
         return go
 
     def split_k(d, r):
@@ -273,21 +286,13 @@
             left_h, left_l, right = [], [], []
             for dx, dz in spots:
                 n = chip(-dx, -dz)
-                left_h.append(mh[n])
-                left_l.append(ml[n])
+                left_h.append((mh if it else nh)[n])
+                left_l.append((ml if it else nl)[n])
                 rows = pl.ds(pl.multiple_of(128 * n, 128), 128)
                 right.append(jnp.concatenate([x2[it, 0, rows], x2[it, 1, rows]], axis=1))
             xh, xl = halves(jnp.concatenate(right, axis=0))
             part[...] += dot3(jnp.concatenate(left_h, axis=1), jnp.concatenate(left_l, axis=1), xh, xl)
         return go
-
-    def boundary_by_node(n):
-        right = []
-        for block in range(2 * n, 2 * n + 4):
-            rows = pl.ds(block % 2 * 32 + block // 2, FACE, stride=FACE)
-            right.append(jnp.concatenate([x2[0, 0, rows], x2[0, 1, rows]], axis=1))
-        xh, xl = halves(jnp.concatenate(right, axis=0))
-        part[...] += dot3(nh[n // 2], nl[n // 2], xh, xl)
 
     def put_x(it, rows):
         for h in range(2):
@@ -342,18 +347,14 @@
             if seen[dx, dz] == 2:
                 share(block)
                 fresh.append((dx, dz))
-            if it and now >= 12 and len(fresh) > LAG:
+            if now >= START[it] and len(fresh) > LAG:
                 early, fresh = fresh[:2], fresh[2:]
                 tasks[:0] = [(0, shared(early)), (0, boundary(it, early))]
             work(now, pops)
         work(99, 99)
         shared(fresh)()
-        if it:
-            for i in range(0, len(fresh), 4):
-                boundary(it, fresh[i : i + 4])()
-        else:
-            for n in range(0, 32, 2):
-                boundary_by_node(n)
+        for i in range(0, len(fresh), 4):
+            boundary(it, fresh[i : i + 4])()
 
     def reduce(it, tasks):
         for i in (2, 1, 3):
@@ -374,7 +375,7 @@
 
     lead.wait()
     put_x(0, exact(node_out, u2[0]))
-    early = [rest.wait] + [copy.wait for copy in get_m] + [split_m(p) for p in range(16)] + [order_m(n) for n in range(16)]
+    early = [rest.wait] + [copy.wait for copy in get_m] + [split_m(p) for p in range(16)] + [turn_m(n) for n in range(32)] + [order_m(n) for n in range(32)]
     later = [get_k.wait] + [split_u(u2, d) for d in range(3)]
     later += [split_k(0, r) for r in range(4)] + [get_l.wait] + [volume(u2, v2, 0, r) for r in range(2)]
     tasks = [(-1, task) for task in early[:13]] + [(0, task) for task in early[13:]]
@@ -386,7 +387,7 @@
         tasks += [(0, split_k(d, r)) for r in range(4)] + [(0, volume(u2, v2, d, r)) for r in range(2)]
         tasks += [(0, faces(0, u, v, u2, v2, d))]
     tasks += [(56, lambda: rows_turn(1))]
-    gather(0, tasks, 3)
+    gather(0, tasks, 4)
     traction = reduce(0, [])
     put_x(1, exact(slot_in, rows_in(1)) - damping * traction)
     tr[...] = traction
@@ -395,8 +396,8 @@
         v2[0] -= damping * exact(node_in, rows_in(2))
         pltpu.make_async_copy(halo.at[0], halo.at[0], hsend.at[0]).wait()
 
-    tasks = [(-1, lambda: rows_out(2, exact(slot_out, tr[...]))), (14, lambda: rows_turn(2))]
-    tasks += [(30, first_top), (30, face_out(1, v))] + [(30, split_u(v2, d)) for d in range(3)]
+    tasks = [(-1, lambda: rows_out(2, exact(slot_out, tr[...]))), (10, lambda: rows_turn(2))]
+    tasks += [(22, first_top), (22, face_out(1, v))] + [(22, split_u(v2, d)) for d in range(3)]
     for d in (2, 1, 0):
         tasks += [(0, volume(v2, u2, d, r)) for r in range(2)]
     gather(1, tasks, 3)
@@ -444,8 +445,8 @@
             pltpu.VMEM((DEPTH, NODES, NODES), F32),
             pltpu.VMEM((DEPTH, NODES, NODES), BF16), pltpu.VMEM((DEPTH, NODES, NODES), BF16),
             pltpu.VMEM((GROUPS, FACE, COLS), F32),
-            *[pltpu.VMEM((32, 256, 128), BF16)] * 2,
-            *[pltpu.VMEM((16, 256, 256), BF16)] * 2,
+            *[pltpu.VMEM((32, 256, 128), BF16)] * 4,
+            pltpu.VMEM((2, COLS, 128), F32),
             pltpu.VMEM((2, 2, 64, FACE, 128), F32),
             pltpu.VMEM((256, FIELDS), F32),
             pltpu.VMEM((2, 3, FACE, FIELDS), F32),

time: 89 us -> 85.9 us (0.965)
  Pallas kernels: 84.9 us -> 81.8 us
    pallas_call x1, Pallas kernels: 84.9 us -> 81.8 us  [shards(): pl.pallas_call(kernel, out_shape=(jax.ShapeDtypeStruct(flat, F32), jax.Sh...]
where the time goes in v3:
time: 85.9 us; the launch traced here: 85.8 us
  Pallas kernels  81.8 us (95%)
  local copies, waits for them, and re-layouts  3.32 us (4%)
    pallas_call x1, Pallas kernels, shards(): pl.pallas_call(kernel, out_shape=(jax.ShapeDtypeStruct(flat, F32), jax.Sh...  81.8 us
    unnamed x4, local copies, waits for them, and re-layouts  3.32 us

profile of v3, /device:TPU:1, one launch (start us, length us, event | category | flops | bytes accessed | tf_op | source)
XLA Modules:
  0.0 85.8 jit_solution(13820547785119267007)
XLA Ops:
  0.6 81.8 %interface_iterations.1 = (f32[3,512,256]{2,1,0:T(8,128)}, f32[64,256]{1,0:T(8,128)}) custom-call(f32[3,512,512]{2,1,0:T(8,128)} %bitcast.6, f32[3,512,256]{2,1,0:T(8,128)} %bitcast.7, f32[3,512,256]{2,1,0:T(8,128)} %bitcast.8, f32[64,4,4096]{2,1,0:T(4,128)} %bm.1, s32[32,128]{1,0:T(8,128)} %bitcast.11), custom_call_target="tpu_custom_call" | custom-call | tf_op jit(solution)/shard_map/interface_iterations/pallas_call | solution.py:434
  82.4 0.0 copy-start
  82.4 2.7 %copy.9 = f32[1,3,512,256]{3,2,1,0:T(8,128)} copy(f32[1,3,512,256]{3,2,1,0:T(8,128)} %bitcast.9) | data formatting | bytes 3145728
  85.1 0.0 copy-done
  85.1 0.6 copy.10
Async XLA Ops:
  82.4 2.7 %copy-start = (f32[64,256]{1,0:T(8,128)S(1)}, f32[64,256]{1,0:T(8,128)}, u32[]{:S(2)}) copy-start(f32[64,256]{1,0:T(8,128)} %get-tuple-element.5) | copy-start | bytes 196612

commit v4 on v3

--- a/solution.py
+++ b/solution.py
@@ -130,7 +130,6 @@
     for i in range(1, GROUPS):
         greet(s, (y + i) % GROUPS)
     greet((s + NX * NZ * NC - sgn) % (NX * NZ * NC), y)
-    pl.semaphore_wait(barrier, NX * NC - 1 + NZ - 1 + GROUPS - 1 + 1)
 
     sub = lax.broadcasted_iota(jnp.int32, (FACE, FACE), 0)
     lane = lax.broadcasted_iota(jnp.int32, (FACE, FACE), 1)
@@ -375,6 +374,7 @@
 
     lead.wait()
     put_x(0, exact(node_out, u2[0]))
+    pl.semaphore_wait(barrier, NX * NC - 1 + NZ - 1 + GROUPS - 1 + 1)
     early = [rest.wait] + [copy.wait for copy in get_m] + [split_m(p) for p in range(16)] + [turn_m(n) for n in range(32)] + [order_m(n) for n in range(32)]
     later = [get_k.wait] + [split_u(u2, d) for d in range(3)]
     later += [split_k(0, r) for r in range(4)] + [get_l.wait] + [volume(u2, v2, 0, r) for r in range(2)]
@@ -402,12 +402,14 @@
         tasks += [(0, volume(v2, u2, d, r)) for r in range(2)]
     gather(1, tasks, 3)
     deep = pltpu.make_async_copy(u2.at[pl.ds(1, 2)], sol.at[pl.ds(1, 2)], osem.at[0])
-    traction = reduce(1, [face_in(1)] + [faces(1, v, u, v2, u2, d) for d in (2, 1, 0)] + [deep.start])
+    traction = reduce(1, [])
     tr[...] = traction
     rows_out(3, exact(slot_out, traction))
     put_tr = pltpu.make_async_copy(tr, trac, osem.at[1])
     put_tr.start()
     rows_turn(3)
+    for task in [face_in(1)] + [faces(1, v, u, v2, u2, d) for d in (2, 1, 0)] + [deep.start]:
+        task()
     u2[0] -= damping * exact(node_in, rows_in(3))
     last = pltpu.make_async_copy(u2.at[0], sol.at[0], osem.at[2])
     last.start()

time: 85.9 us -> 85.5 us (level)
  no operation moved by 1% of the time
where the time goes in v4:
time: 85.5 us; the launch traced here: 85.3 us
  Pallas kernels  81.4 us (95%)
  local copies, waits for them, and re-layouts  3.32 us (4%)
    pallas_call x1, Pallas kernels, shards(): pl.pallas_call(kernel, out_shape=(jax.ShapeDtypeStruct(flat, F32), jax.Sh...  81.4 us
    unnamed x4, local copies, waits for them, and re-layouts  3.32 us

profile of v4, /device:TPU:1, one launch (start us, length us, event | category | flops | bytes accessed | tf_op | source)
XLA Modules:
  0.0 85.3 jit_solution(8014196923923522827)
XLA Ops:
  0.6 81.4 %interface_iterations.1 = (f32[3,512,256]{2,1,0:T(8,128)}, f32[64,256]{1,0:T(8,128)}) custom-call(f32[3,512,512]{2,1,0:T(8,128)} %bitcast.6, f32[3,512,256]{2,1,0:T(8,128)} %bitcast.7, f32[3,512,256]{2,1,0:T(8,128)} %bitcast.8, f32[64,4,4096]{2,1,0:T(4,128)} %bm.1, s32[32,128]{1,0:T(8,128)} %bitcast.11), custom_call_target="tpu_custom_call" | custom-call | tf_op jit(solution)/shard_map/interface_iterations/pallas_call | solution.py:436
  82.0 0.0 copy-start
  82.0 2.7 %copy.9 = f32[1,3,512,256]{3,2,1,0:T(8,128)} copy(f32[1,3,512,256]{3,2,1,0:T(8,128)} %bitcast.9) | data formatting | bytes 3145728
  84.7 0.0 copy-done
  84.7 0.6 copy.10
Async XLA Ops:
  82.0 2.7 %copy-start = (f32[64,256]{1,0:T(8,128)S(1)}, f32[64,256]{1,0:T(8,128)}, u32[]{:S(2)}) copy-start(f32[64,256]{1,0:T(8,128)} %get-tuple-element.5) | copy-start | bytes 196612

commit v5 on v4

--- a/solution.py
+++ b/solution.py
@@ -10,7 +10,7 @@
 MESH = pl.DeviceIdType.MESH
 F32, BF16 = jnp.float32, jnp.bfloat16
 START = (30, 12)
-LAG = 8
+LAG = 5
 NX, NZ, NC = 4, 8, 2
 EDGE, DEPTH, NODES, FACE, FIELDS = 8, 3, 512, 64, 256
 GROUPS, COLS = 4, 4096

time: 85.5 us -> 86 us (level)
  no operation moved by 1% of the time
where the time goes in v5:
time: 86 us; the launch traced here: 85.8 us
  Pallas kernels  81.8 us (95%)
  local copies, waits for them, and re-layouts  3.32 us (4%)
    pallas_call x1, Pallas kernels, shards(): pl.pallas_call(kernel, out_shape=(jax.ShapeDtypeStruct(flat, F32), jax.Sh...  81.8 us
    unnamed x4, local copies, waits for them, and re-layouts  3.32 us

profile of v5, /device:TPU:1, one launch (start us, length us, event | category | flops | bytes accessed | tf_op | source)
XLA Modules:
  0.0 85.8 jit_solution(10748361518611320884)
XLA Ops:
  0.6 81.8 %interface_iterations.1 = (f32[3,512,256]{2,1,0:T(8,128)}, f32[64,256]{1,0:T(8,128)}) custom-call(f32[3,512,512]{2,1,0:T(8,128)} %bitcast.6, f32[3,512,256]{2,1,0:T(8,128)} %bitcast.7, f32[3,512,256]{2,1,0:T(8,128)} %bitcast.8, f32[64,4,4096]{2,1,0:T(4,128)} %bm.1, s32[32,128]{1,0:T(8,128)} %bitcast.11), custom_call_target="tpu_custom_call" | custom-call | tf_op jit(solution)/shard_map/interface_iterations/pallas_call | solution.py:436
  82.5 0.0 copy-start
  82.5 2.7 %copy.9 = f32[1,3,512,256]{3,2,1,0:T(8,128)} copy(f32[1,3,512,256]{3,2,1,0:T(8,128)} %bitcast.9) | data formatting | bytes 3145728
  85.2 0.0 copy-done
  85.2 0.6 copy.10
Async XLA Ops:
  82.5 2.7 %copy-start = (f32[64,256]{1,0:T(8,128)S(1)}, f32[64,256]{1,0:T(8,128)}, u32[]{:S(2)}) copy-start(f32[64,256]{1,0:T(8,128)} %get-tuple-element.5) | copy-start | bytes 196612
